TPU v7x, 32 devices: a whole 2x2x4 slice. The times are simulated.
32 devices in a mesh: groups: 2 (over x), tm: 16 (over z, y, core).
Axes of the slice: x: 2, y: 2, z: 4, core: 2. Of those that a mesh axis runs over, the one named last changes fastest.
Arguments:
- points: float32 [32, 64, 2048], P(('groups', 'tm')), parts along dimension 0, may hold values from -4 to 4
- potentials: float32 [32, 224, 2048], P(('groups', 'tm')), parts along dimension 0, may hold values from 0.5 to 25, as said below
- supports: int32 [32], P(('groups', 'tm')), parts along dimension 0, may hold values from 512 to 2048, as said below
Outputs:
- messages: float32 [32, 224, 2048], P(('groups', 'tm')), parts along dimension 0
- log_scale: float32 [448], P('groups'), parts along dimension 0
There are 2 independent parts, one for each index of `groups`. A program takes and returns all parts, laid end to end along the dimension named above; each array names one. Nothing has to cross between parts.
Inputs may be any that keep to these rules, and one draw needn't show every extreme that they name: `supports`: the first and the last time slice have all 2048 points live; every other slice has between 512 and 1024 live points, at its first positions. `potentials`: positive scalings.
All inputs are finite; a program needn't handle non-finite values.
Results may differ from a plain program's by a relative error of at most 0.017.
Values may be sent and summed in bfloat16 or wider, within the bound.
A program may use at most 64 MiB of HBM per device.

v0:
```python
import jax
import jax.numpy as jnp
from jax import lax
from jax.sharding import PartitionSpec as P

MICRO = 32


A_DECAY = 0.8
EPS_SCALE = 0.05


def shifted(value, axis, steps):
    count = lax.axis_size(axis)
    initial, last = (max(0, -steps), min(count, count - steps))
    return lax.ppermute(value, axis, [(source, source + steps) for source in range(initial, last)])


def slice_kernel(source, target):
    dim_count, point_count = source.shape
    block_rows = min(512, point_count)
    inv_width = 1.0 / (2.0 * EPS_SCALE * dim_count)
    target_sq = jnp.sum(target * target, axis=0)
    pieces = jnp.transpose(
        source.reshape(dim_count, point_count // block_rows, block_rows), (1, 0, 2)
    )

    def one_block(segment):
        products = lax.dot_general(
            segment,
            target,
            (((0,), (0,)), ((), ())),
            precision=lax.Precision.HIGHEST,
            preferred_element_type=jnp.float32,
        )
        segment_sq = jnp.sum(segment * segment, axis=0)
        distance = (
            target_sq[None, :] + A_DECAY * A_DECAY * segment_sq[:, None] - 2.0 * A_DECAY * products
        )
        return jnp.exp(-inv_width * distance).astype(jnp.bfloat16)

    return lax.map(one_block, pieces).reshape(point_count, point_count)


def push_forward(weighted, kernel, live_row):
    pushed = jnp.dot(weighted, kernel, preferred_element_type=jnp.float32) * live_row[None, :]
    return (pushed, jnp.sum(pushed, axis=1))


def per_device(points, potentials, supports):
    local_slices, dim_count, point_count = points.shape
    all_cols = potentials.shape[1]
    tm_count = lax.axis_size("tm")
    position = lax.axis_index("tm")
    live_mask = (jnp.arange(point_count, dtype=jnp.int32)[None, :] < supports[:, None]).astype(
        jnp.float32
    )
    counts = supports.astype(jnp.float32)
    arrived = shifted(points[local_slices - 1], "tm", 1)
    sources = jnp.concatenate([arrived[None], points[:-1]], axis=0)
    kernels = lax.map(lambda paired: slice_kernel(paired[0], paired[1]), (sources, points))
    block_cols = MICRO
    batches = all_cols // block_cols
    phase_count = tm_count + batches - 1
    is_first = position == 0

    def section(incoming, block_id):
        block_pot = lax.dynamic_slice_in_dim(potentials, block_id * block_cols, block_cols, 1)
        pushed, column_sum = push_forward(incoming, kernels[0], live_mask[0])
        safe_sum = jnp.where(is_first, 1.0, column_sum)
        start_msg = jnp.broadcast_to(live_mask[0][None, :], pushed.shape)
        message = jnp.where(is_first, start_msg, pushed * (counts[0] / safe_sum)[:, None])
        outputs = [message]
        log_terms = [jnp.where(is_first, 0.0, jnp.log(safe_sum / counts[0]))]
        outgoing = (message * block_pot[local_slices - 1]).astype(jnp.bfloat16)
        return (jnp.stack(outputs), jnp.stack(log_terms), outgoing)

    def advance(phase, state_in):
        incoming, messages, log_parts = state_in
        block_id = phase - position
        active = (block_id >= 0) & (block_id < batches)
        clipped = jnp.clip(block_id, 0, batches - 1)

        def compute(operands):
            stored, stored_logs = operands
            block_msgs, block_logs, outgoing = section(incoming, clipped)
            stored = lax.dynamic_update_slice_in_dim(stored, block_msgs, clipped * block_cols, 1)
            stored_logs = lax.dynamic_update_slice_in_dim(
                stored_logs, block_logs, clipped * block_cols, 1
            )
            return (stored, stored_logs, outgoing)

        def skipped(operands):
            stored, stored_logs = operands
            return (stored, stored_logs, jnp.zeros((block_cols, point_count), jnp.bfloat16))

        messages, log_parts, outgoing = lax.cond(active, compute, skipped, (messages, log_parts))
        received = shifted(outgoing, "tm", 1)
        return (received, messages, log_parts)

    initial = (
        jnp.zeros((block_cols, point_count), jnp.bfloat16),
        jnp.zeros((local_slices, all_cols, point_count), jnp.float32),
        jnp.zeros((local_slices, all_cols), jnp.float32),
    )
    unused, messages, log_parts = lax.fori_loop(0, phase_count, advance, initial)
    local_log = jnp.sum(log_parts, axis=0)
    log_scale = lax.psum(local_log, "tm") / (tm_count * local_slices - 1)
    return (messages, log_scale)


def solution(mesh):
    placed = (P(("groups", "tm"), None, None), P(("groups", "tm"), None, None), P(("groups", "tm")))
    return jax.shard_map(
        per_device,
        mesh=mesh,
        in_specs=placed,
        out_specs=(P(("groups", "tm"), None, None), P("groups")),
        check_vma=False,
    )
```

profile of v0, /device:TPU:0, one launch (start us, length us, event | category | flops | bytes accessed | tf_op | source)
XLA Modules:
  0.0 334.7 jit_solution(13703646366627489090)
XLA Ops:
  0.6 2.4 collective-permute-start.1
  3.7 1.1 multiply_reduce_fusion
  4.8 26.2 %while.35 = (s32[]{:T(128)}, bf16[4,512,2048]{2,1,0:T(8,128)(2,1)}, f32[2048]{0:T(1024)S(1)}, f32[4,64,512]{2,1,0:T(8,128)S(1)}, f32[64,2048]{1,0:T(8,128)}, /*index=5*/s32[]{:T(128)}) while((s32[]{:T(128)}, bf16[4,512,2048]{2,1,0:T(8,128)(2,1)}, f32[2048]{0:T(1024)S(1)}, f32[4,64,512]{2,1,0:T(8,128)S(1)}, f32[64,2048]{1,0:T(8,128)}, ...), condition=%wide.region_3.0_spmd, body=%wide.region_1.3_spmd.sunk | while | flops 810614784 | bytes 2901065 | solution.py:42
  4.9 6.6 %fusion.26 = bf16[4,512,2048]{2,1,0:T(8,128)(2,1)} fusion(bf16[4,512,2048]{2,1,0:T(8,128)(2,1)} %get-tuple-element.449, s32[]{:T(128)} %get-tuple-element.448, f32[64,2048]{1,0:T(8,128)} %get-tuple-element.458, f32[512]{0:T(512)S(1)} %broadcast_multiply_fusion.3, f32[2048]{0:T(1024)S(1)} %get-tuple-element.456, f32[4,64,512]{2,1,0:T(8,128)S(1)} %get-tuple-element.457), kind=kOutput, calls=%fused_computation.3.clone.1 | convolution fusion | flops 810549248 | bytes 2763776 | tf_op jit(solution)/shard_map/while/body/eval_jaxpr/while/body/eval_jaxpr/dot_general | solution.py:29
  11.5 6.5 %fusion.26 = bf16[4,512,2048]{2,1,0:T(8,128)(2,1)} fusion(bf16[4,512,2048]{2,1,0:T(8,128)(2,1)} %get-tuple-element.449, s32[]{:T(128)} %get-tuple-element.448, f32[64,2048]{1,0:T(8,128)} %get-tuple-element.458, f32[512]{0:T(512)S(1)} %broadcast_multiply_fusion.3, f32[2048]{0:T(1024)S(1)} %get-tuple-element.456, f32[4,64,512]{2,1,0:T(8,128)S(1)} %get-tuple-element.457), kind=kOutput, calls=%fused_computation.3.clone.1 | convolution fusion | flops 810549248 | bytes 2763776 | tf_op jit(solution)/shard_map/while/body/eval_jaxpr/while/body/eval_jaxpr/dot_general | solution.py:29
  18.0 6.5 %fusion.26 = bf16[4,512,2048]{2,1,0:T(8,128)(2,1)} fusion(bf16[4,512,2048]{2,1,0:T(8,128)(2,1)} %get-tuple-element.449, s32[]{:T(128)} %get-tuple-element.448, f32[64,2048]{1,0:T(8,128)} %get-tuple-element.458, f32[512]{0:T(512)S(1)} %broadcast_multiply_fusion.3, f32[2048]{0:T(1024)S(1)} %get-tuple-element.456, f32[4,64,512]{2,1,0:T(8,128)S(1)} %get-tuple-element.457), kind=kOutput, calls=%fused_computation.3.clone.1 | convolution fusion | flops 810549248 | bytes 2763776 | tf_op jit(solution)/shard_map/while/body/eval_jaxpr/while/body/eval_jaxpr/dot_general | solution.py:29
  24.6 6.5 %fusion.26 = bf16[4,512,2048]{2,1,0:T(8,128)(2,1)} fusion(bf16[4,512,2048]{2,1,0:T(8,128)(2,1)} %get-tuple-element.449, s32[]{:T(128)} %get-tuple-element.448, f32[64,2048]{1,0:T(8,128)} %get-tuple-element.458, f32[512]{0:T(512)S(1)} %broadcast_multiply_fusion.3, f32[2048]{0:T(1024)S(1)} %get-tuple-element.456, f32[4,64,512]{2,1,0:T(8,128)S(1)} %get-tuple-element.457), kind=kOutput, calls=%fused_computation.3.clone.1 | convolution fusion | flops 810549248 | bytes 2763776 | tf_op jit(solution)/shard_map/while/body/eval_jaxpr/while/body/eval_jaxpr/dot_general | solution.py:29
  31.3 226.2 %while.36 = (s32[]{:T(128)}, bf16[32,2048]{1,0:T(8,128)(2,1)S(1)}, f32[1,224,2048]{2,1,0:T(8,128)S(1)}, f32[1,224]{1,0:T(1,128)S(1)}, s32[]{:T(128)}, /*index=5*...) while((s32[]{:T(128)}, bf16[32,2048]{1,0:T(8,128)(2,1)S(1)}, ...), condition=%wide.region_8.9_spmd.clone, body=%wide.region_4.8_spmd.clone.sunk | while | flops 268963936 | bytes 10520344 | solution.py:106
  32.0 6.4 %conditional.3 = (f32[1,224,2048]{2,1,0:T(8,128)S(1)}, f32[1,224]{1,0:T(1,128)S(1)}, bf16[32,2048]{1,0:T(8,128)(2,1)S(1)}) conditional(s32[]{:T(128)} %convert_element_type.47, (f32[1,224,2048]{2,1,0:T(8,128)S(1)}, f32[1,224]{1,0:T(1,128)S(1)}) %tuple.68, (pred[]{:T(512)}, f32[1,2048]{1,0:T(1,128)S(1)}, bf16[1,2048,2048]{2,1,0:T(8,128)(2,1)}, ...), branch_computations={%region_5.5_spmd, %region_6.7_spmd} | conditional | flops 268959840 | bytes 9987569 | solution.py:97
  32.0 5.0 %fusion.16 = (f32[32]{0:T(128)S(1)}, f32[32,2048]{1,0:T(8,128)S(1)}) fusion(f32[2048]{0:T(1024)S(1)} %bitcast.50, bf16[32,2048]{1,0:T(8,128)(2,1)S(1)} %get-tuple-element.250, bf16[1,2048,2048]{2,1,0:T(8,128)(2,1)} %get-tuple-element.251), kind=kOutput, calls=%fused_computation.25 | convolution fusion | flops 268566496 | bytes 8790144 | tf_op jit(solution)/shard_map/while/body/eval_jaxpr/cond/branch_1_fun/dot_general | solution.py:46
  37.2 1.1 fusion.13
  38.4 2.8 collective-permute-start
  41.2 1.0 collective-permute-done
  42.9 6.5 %conditional.3 = (f32[1,224,2048]{2,1,0:T(8,128)S(1)}, f32[1,224]{1,0:T(1,128)S(1)}, bf16[32,2048]{1,0:T(8,128)(2,1)S(1)}) conditional(s32[]{:T(128)} %convert_element_type.47, (f32[1,224,2048]{2,1,0:T(8,128)S(1)}, f32[1,224]{1,0:T(1,128)S(1)}) %tuple.68, (pred[]{:T(512)}, f32[1,2048]{1,0:T(1,128)S(1)}, bf16[1,2048,2048]{2,1,0:T(8,128)(2,1)}, ...), branch_computations={%region_5.5_spmd, %region_6.7_spmd} | conditional | flops 268959840 | bytes 9987569 | solution.py:97
  42.9 5.0 %fusion.16 = (f32[32]{0:T(128)S(1)}, f32[32,2048]{1,0:T(8,128)S(1)}) fusion(f32[2048]{0:T(1024)S(1)} %bitcast.50, bf16[32,2048]{1,0:T(8,128)(2,1)S(1)} %get-tuple-element.250, bf16[1,2048,2048]{2,1,0:T(8,128)(2,1)} %get-tuple-element.251), kind=kOutput, calls=%fused_computation.25 | convolution fusion | flops 268566496 | bytes 8790144 | tf_op jit(solution)/shard_map/while/body/eval_jaxpr/cond/branch_1_fun/dot_general | solution.py:46
  48.0 1.1 fusion.13
  49.4 5.2 %collective-permute-start = (bf16[32,2048]{1,0:T(8,128)(2,1)S(1)}, bf16[32,2048]{1,0:T(8,128)(2,1)S(1)}, u32[]{:S(2)}, u32[]{:S(2)}) collective-permute-start(bf16[32,2048]{1,0:T(8,128)(2,1)S(1)} %get-tuple-element.433), channel_id=1, source_target_pairs={{0,1},{1,2},{2,3},{3,4},{4,5},{5,6},{6,7},{7,8},{8,9},{9,10},{10,1... | collective-permute-start | bytes 393224 | tf_op jit(solution)/shard_map/while/body/eval_jaxpr/ppermute | solution.py:16
  54.5 1.0 collective-permute-done
  56.2 6.5 %conditional.3 = (f32[1,224,2048]{2,1,0:T(8,128)S(1)}, f32[1,224]{1,0:T(1,128)S(1)}, bf16[32,2048]{1,0:T(8,128)(2,1)S(1)}) conditional(s32[]{:T(128)} %convert_element_type.47, (f32[1,224,2048]{2,1,0:T(8,128)S(1)}, f32[1,224]{1,0:T(1,128)S(1)}) %tuple.68, (pred[]{:T(512)}, f32[1,2048]{1,0:T(1,128)S(1)}, bf16[1,2048,2048]{2,1,0:T(8,128)(2,1)}, ...), branch_computations={%region_5.5_spmd, %region_6.7_spmd} | conditional | flops 268959840 | bytes 9987569 | solution.py:97
  56.2 5.0 %fusion.16 = (f32[32]{0:T(128)S(1)}, f32[32,2048]{1,0:T(8,128)S(1)}) fusion(f32[2048]{0:T(1024)S(1)} %bitcast.50, bf16[32,2048]{1,0:T(8,128)(2,1)S(1)} %get-tuple-element.250, bf16[1,2048,2048]{2,1,0:T(8,128)(2,1)} %get-tuple-element.251), kind=kOutput, calls=%fused_computation.25 | convolution fusion | flops 268566496 | bytes 8790144 | tf_op jit(solution)/shard_map/while/body/eval_jaxpr/cond/branch_1_fun/dot_general | solution.py:46
  61.4 1.1 fusion.13
  62.7 2.9 collective-permute-start
  65.6 1.0 collective-permute-done
  67.2 6.5 %conditional.3 = (f32[1,224,2048]{2,1,0:T(8,128)S(1)}, f32[1,224]{1,0:T(1,128)S(1)}, bf16[32,2048]{1,0:T(8,128)(2,1)S(1)}) conditional(s32[]{:T(128)} %convert_element_type.47, (f32[1,224,2048]{2,1,0:T(8,128)S(1)}, f32[1,224]{1,0:T(1,128)S(1)}) %tuple.68, (pred[]{:T(512)}, f32[1,2048]{1,0:T(1,128)S(1)}, bf16[1,2048,2048]{2,1,0:T(8,128)(2,1)}, ...), branch_computations={%region_5.5_spmd, %region_6.7_spmd} | conditional | flops 268959840 | bytes 9987569 | solution.py:97
  67.3 5.0 %fusion.16 = (f32[32]{0:T(128)S(1)}, f32[32,2048]{1,0:T(8,128)S(1)}) fusion(f32[2048]{0:T(1024)S(1)} %bitcast.50, bf16[32,2048]{1,0:T(8,128)(2,1)S(1)} %get-tuple-element.250, bf16[1,2048,2048]{2,1,0:T(8,128)(2,1)} %get-tuple-element.251), kind=kOutput, calls=%fused_computation.25 | convolution fusion | flops 268566496 | bytes 8790144 | tf_op jit(solution)/shard_map/while/body/eval_jaxpr/cond/branch_1_fun/dot_general | solution.py:46
  72.4 1.1 fusion.13
  73.7 5.2 %collective-permute-start = (bf16[32,2048]{1,0:T(8,128)(2,1)S(1)}, bf16[32,2048]{1,0:T(8,128)(2,1)S(1)}, u32[]{:S(2)}, u32[]{:S(2)}) collective-permute-start(bf16[32,2048]{1,0:T(8,128)(2,1)S(1)} %get-tuple-element.433), channel_id=1, source_target_pairs={{0,1},{1,2},{2,3},{3,4},{4,5},{5,6},{6,7},{7,8},{8,9},{9,10},{10,1... | collective-permute-start | bytes 393224 | tf_op jit(solution)/shard_map/while/body/eval_jaxpr/ppermute | solution.py:16
  79.0 1.0 collective-permute-done
  80.6 6.4 %conditional.3 = (f32[1,224,2048]{2,1,0:T(8,128)S(1)}, f32[1,224]{1,0:T(1,128)S(1)}, bf16[32,2048]{1,0:T(8,128)(2,1)S(1)}) conditional(s32[]{:T(128)} %convert_element_type.47, (f32[1,224,2048]{2,1,0:T(8,128)S(1)}, f32[1,224]{1,0:T(1,128)S(1)}) %tuple.68, (pred[]{:T(512)}, f32[1,2048]{1,0:T(1,128)S(1)}, bf16[1,2048,2048]{2,1,0:T(8,128)(2,1)}, ...), branch_computations={%region_5.5_spmd, %region_6.7_spmd} | conditional | flops 268959840 | bytes 9987569 | solution.py:97
  80.6 5.0 %fusion.16 = (f32[32]{0:T(128)S(1)}, f32[32,2048]{1,0:T(8,128)S(1)}) fusion(f32[2048]{0:T(1024)S(1)} %bitcast.50, bf16[32,2048]{1,0:T(8,128)(2,1)S(1)} %get-tuple-element.250, bf16[1,2048,2048]{2,1,0:T(8,128)(2,1)} %get-tuple-element.251), kind=kOutput, calls=%fused_computation.25 | convolution fusion | flops 268566496 | bytes 8790144 | tf_op jit(solution)/shard_map/while/body/eval_jaxpr/cond/branch_1_fun/dot_general | solution.py:46
  85.8 1.1 fusion.13
  87.0 5.4 %collective-permute-start = (bf16[32,2048]{1,0:T(8,128)(2,1)S(1)}, bf16[32,2048]{1,0:T(8,128)(2,1)S(1)}, u32[]{:S(2)}, u32[]{:S(2)}) collective-permute-start(bf16[32,2048]{1,0:T(8,128)(2,1)S(1)} %get-tuple-element.433), channel_id=1, source_target_pairs={{0,1},{1,2},{2,3},{3,4},{4,5},{5,6},{6,7},{7,8},{8,9},{9,10},{10,1... | collective-permute-start | bytes 393224 | tf_op jit(solution)/shard_map/while/body/eval_jaxpr/ppermute | solution.py:16
  92.5 1.0 collective-permute-done
  94.1 6.5 %conditional.3 = (f32[1,224,2048]{2,1,0:T(8,128)S(1)}, f32[1,224]{1,0:T(1,128)S(1)}, bf16[32,2048]{1,0:T(8,128)(2,1)S(1)}) conditional(s32[]{:T(128)} %convert_element_type.47, (f32[1,224,2048]{2,1,0:T(8,128)S(1)}, f32[1,224]{1,0:T(1,128)S(1)}) %tuple.68, (pred[]{:T(512)}, f32[1,2048]{1,0:T(1,128)S(1)}, bf16[1,2048,2048]{2,1,0:T(8,128)(2,1)}, ...), branch_computations={%region_5.5_spmd, %region_6.7_spmd} | conditional | flops 268959840 | bytes 9987569 | solution.py:97
  94.1 5.0 %fusion.16 = (f32[32]{0:T(128)S(1)}, f32[32,2048]{1,0:T(8,128)S(1)}) fusion(f32[2048]{0:T(1024)S(1)} %bitcast.50, bf16[32,2048]{1,0:T(8,128)(2,1)S(1)} %get-tuple-element.250, bf16[1,2048,2048]{2,1,0:T(8,128)(2,1)} %get-tuple-element.251), kind=kOutput, calls=%fused_computation.25 | convolution fusion | flops 268566496 | bytes 8790144 | tf_op jit(solution)/shard_map/while/body/eval_jaxpr/cond/branch_1_fun/dot_general | solution.py:46
  99.3 1.1 fusion.13
  100.6 5.2 %collective-permute-start = (bf16[32,2048]{1,0:T(8,128)(2,1)S(1)}, bf16[32,2048]{1,0:T(8,128)(2,1)S(1)}, u32[]{:S(2)}, u32[]{:S(2)}) collective-permute-start(bf16[32,2048]{1,0:T(8,128)(2,1)S(1)} %get-tuple-element.433), channel_id=1, source_target_pairs={{0,1},{1,2},{2,3},{3,4},{4,5},{5,6},{6,7},{7,8},{8,9},{9,10},{10,1... | collective-permute-start | bytes 393224 | tf_op jit(solution)/shard_map/while/body/eval_jaxpr/ppermute | solution.py:16
  105.8 1.0 collective-permute-done
  107.5 6.5 %conditional.3 = (f32[1,224,2048]{2,1,0:T(8,128)S(1)}, f32[1,224]{1,0:T(1,128)S(1)}, bf16[32,2048]{1,0:T(8,128)(2,1)S(1)}) conditional(s32[]{:T(128)} %convert_element_type.47, (f32[1,224,2048]{2,1,0:T(8,128)S(1)}, f32[1,224]{1,0:T(1,128)S(1)}) %tuple.68, (pred[]{:T(512)}, f32[1,2048]{1,0:T(1,128)S(1)}, bf16[1,2048,2048]{2,1,0:T(8,128)(2,1)}, ...), branch_computations={%region_5.5_spmd, %region_6.7_spmd} | conditional | flops 268959840 | bytes 9987569 | solution.py:97
  107.5 5.0 %fusion.16 = (f32[32]{0:T(128)S(1)}, f32[32,2048]{1,0:T(8,128)S(1)}) fusion(f32[2048]{0:T(1024)S(1)} %bitcast.50, bf16[32,2048]{1,0:T(8,128)(2,1)S(1)} %get-tuple-element.250, bf16[1,2048,2048]{2,1,0:T(8,128)(2,1)} %get-tuple-element.251), kind=kOutput, calls=%fused_computation.25 | convolution fusion | flops 268566496 | bytes 8790144 | tf_op jit(solution)/shard_map/while/body/eval_jaxpr/cond/branch_1_fun/dot_general | solution.py:46
  112.7 1.1 fusion.13
  114.0 5.4 %collective-permute-start = (bf16[32,2048]{1,0:T(8,128)(2,1)S(1)}, bf16[32,2048]{1,0:T(8,128)(2,1)S(1)}, u32[]{:S(2)}, u32[]{:S(2)}) collective-permute-start(bf16[32,2048]{1,0:T(8,128)(2,1)S(1)} %get-tuple-element.433), channel_id=1, source_target_pairs={{0,1},{1,2},{2,3},{3,4},{4,5},{5,6},{6,7},{7,8},{8,9},{9,10},{10,1... | collective-permute-start | bytes 393224 | tf_op jit(solution)/shard_map/while/body/eval_jaxpr/ppermute | solution.py:16
  121.1 11.7 %collective-permute-start = (bf16[32,2048]{1,0:T(8,128)(2,1)S(1)}, bf16[32,2048]{1,0:T(8,128)(2,1)S(1)}, u32[]{:S(2)}, u32[]{:S(2)}) collective-permute-start(bf16[32,2048]{1,0:T(8,128)(2,1)S(1)} %get-tuple-element.433), channel_id=1, source_target_pairs={{0,1},{1,2},{2,3},{3,4},{4,5},{5,6},{6,7},{7,8},{8,9},{9,10},{10,1... | collective-permute-start | bytes 393224 | tf_op jit(solution)/shard_map/while/body/eval_jaxpr/ppermute | solution.py:16
  132.8 1.0 collective-permute-done
  134.5 5.3 %collective-permute-start = (bf16[32,2048]{1,0:T(8,128)(2,1)S(1)}, bf16[32,2048]{1,0:T(8,128)(2,1)S(1)}, u32[]{:S(2)}, u32[]{:S(2)}) collective-permute-start(bf16[32,2048]{1,0:T(8,128)(2,1)S(1)} %get-tuple-element.433), channel_id=1, source_target_pairs={{0,1},{1,2},{2,3},{3,4},{4,5},{5,6},{6,7},{7,8},{8,9},{9,10},{10,1... | collective-permute-start | bytes 393224 | tf_op jit(solution)/shard_map/while/body/eval_jaxpr/ppermute | solution.py:16
  139.8 1.0 collective-permute-done
  141.5 11.8 %collective-permute-start = (bf16[32,2048]{1,0:T(8,128)(2,1)S(1)}, bf16[32,2048]{1,0:T(8,128)(2,1)S(1)}, u32[]{:S(2)}, u32[]{:S(2)}) collective-permute-start(bf16[32,2048]{1,0:T(8,128)(2,1)S(1)} %get-tuple-element.433), channel_id=1, source_target_pairs={{0,1},{1,2},{2,3},{3,4},{4,5},{5,6},{6,7},{7,8},{8,9},{9,10},{10,1... | collective-permute-start | bytes 393224 | tf_op jit(solution)/shard_map/while/body/eval_jaxpr/ppermute | solution.py:16
  154.9 5.3 %collective-permute-start = (bf16[32,2048]{1,0:T(8,128)(2,1)S(1)}, bf16[32,2048]{1,0:T(8,128)(2,1)S(1)}, u32[]{:S(2)}, u32[]{:S(2)}) collective-permute-start(bf16[32,2048]{1,0:T(8,128)(2,1)S(1)} %get-tuple-element.433), channel_id=1, source_target_pairs={{0,1},{1,2},{2,3},{3,4},{4,5},{5,6},{6,7},{7,8},{8,9},{9,10},{10,1... | collective-permute-start | bytes 393224 | tf_op jit(solution)/shard_map/while/body/eval_jaxpr/ppermute | solution.py:16
  160.3 1.0 collective-permute-done
  161.9 7.3 %collective-permute-start = (bf16[32,2048]{1,0:T(8,128)(2,1)S(1)}, bf16[32,2048]{1,0:T(8,128)(2,1)S(1)}, u32[]{:S(2)}, u32[]{:S(2)}) collective-permute-start(bf16[32,2048]{1,0:T(8,128)(2,1)S(1)} %get-tuple-element.433), channel_id=1, source_target_pairs={{0,1},{1,2},{2,3},{3,4},{4,5},{5,6},{6,7},{7,8},{8,9},{9,10},{10,1... | collective-permute-start | bytes 393224 | tf_op jit(solution)/shard_map/while/body/eval_jaxpr/ppermute | solution.py:16
  170.9 6.2 %collective-permute-start = (bf16[32,2048]{1,0:T(8,128)(2,1)S(1)}, bf16[32,2048]{1,0:T(8,128)(2,1)S(1)}, u32[]{:S(2)}, u32[]{:S(2)}) collective-permute-start(bf16[32,2048]{1,0:T(8,128)(2,1)S(1)} %get-tuple-element.433), channel_id=1, source_target_pairs={{0,1},{1,2},{2,3},{3,4},{4,5},{5,6},{6,7},{7,8},{8,9},{9,10},{10,1... | collective-permute-start | bytes 393224 | tf_op jit(solution)/shard_map/while/body/eval_jaxpr/ppermute | solution.py:16
  178.8 12.7 %collective-permute-start = (bf16[32,2048]{1,0:T(8,128)(2,1)S(1)}, bf16[32,2048]{1,0:T(8,128)(2,1)S(1)}, u32[]{:S(2)}, u32[]{:S(2)}) collective-permute-start(bf16[32,2048]{1,0:T(8,128)(2,1)S(1)} %get-tuple-element.433), channel_id=1, source_target_pairs={{0,1},{1,2},{2,3},{3,4},{4,5},{5,6},{6,7},{7,8},{8,9},{9,10},{10,1... | collective-permute-start | bytes 393224 | tf_op jit(solution)/shard_map/while/body/eval_jaxpr/ppermute | solution.py:16
  193.2 6.2 %collective-permute-start = (bf16[32,2048]{1,0:T(8,128)(2,1)S(1)}, bf16[32,2048]{1,0:T(8,128)(2,1)S(1)}, u32[]{:S(2)}, u32[]{:S(2)}) collective-permute-start(bf16[32,2048]{1,0:T(8,128)(2,1)S(1)} %get-tuple-element.433), channel_id=1, source_target_pairs={{0,1},{1,2},{2,3},{3,4},{4,5},{5,6},{6,7},{7,8},{8,9},{9,10},{10,1... | collective-permute-start | bytes 393224 | tf_op jit(solution)/shard_map/while/body/eval_jaxpr/ppermute | solution.py:16
  201.1 6.2 %collective-permute-start = (bf16[32,2048]{1,0:T(8,128)(2,1)S(1)}, bf16[32,2048]{1,0:T(8,128)(2,1)S(1)}, u32[]{:S(2)}, u32[]{:S(2)}) collective-permute-start(bf16[32,2048]{1,0:T(8,128)(2,1)S(1)} %get-tuple-element.433), channel_id=1, source_target_pairs={{0,1},{1,2},{2,3},{3,4},{4,5},{5,6},{6,7},{7,8},{8,9},{9,10},{10,1... | collective-permute-start | bytes 393224 | tf_op jit(solution)/shard_map/while/body/eval_jaxpr/ppermute | solution.py:16
  209.0 6.2 %collective-permute-start = (bf16[32,2048]{1,0:T(8,128)(2,1)S(1)}, bf16[32,2048]{1,0:T(8,128)(2,1)S(1)}, u32[]{:S(2)}, u32[]{:S(2)}) collective-permute-start(bf16[32,2048]{1,0:T(8,128)(2,1)S(1)} %get-tuple-element.433), channel_id=1, source_target_pairs={{0,1},{1,2},{2,3},{3,4},{4,5},{5,6},{6,7},{7,8},{8,9},{9,10},{10,1... | collective-permute-start | bytes 393224 | tf_op jit(solution)/shard_map/while/body/eval_jaxpr/ppermute | solution.py:16
  216.9 6.7 %collective-permute-start = (bf16[32,2048]{1,0:T(8,128)(2,1)S(1)}, bf16[32,2048]{1,0:T(8,128)(2,1)S(1)}, u32[]{:S(2)}, u32[]{:S(2)}) collective-permute-start(bf16[32,2048]{1,0:T(8,128)(2,1)S(1)} %get-tuple-element.433), channel_id=1, source_target_pairs={{0,1},{1,2},{2,3},{3,4},{4,5},{5,6},{6,7},{7,8},{8,9},{9,10},{10,1... | collective-permute-start | bytes 393224 | tf_op jit(solution)/shard_map/while/body/eval_jaxpr/ppermute | solution.py:16
  223.6 1.0 collective-permute-done
  225.2 6.2 %collective-permute-start = (bf16[32,2048]{1,0:T(8,128)(2,1)S(1)}, bf16[32,2048]{1,0:T(8,128)(2,1)S(1)}, u32[]{:S(2)}, u32[]{:S(2)}) collective-permute-start(bf16[32,2048]{1,0:T(8,128)(2,1)S(1)} %get-tuple-element.433), channel_id=1, source_target_pairs={{0,1},{1,2},{2,3},{3,4},{4,5},{5,6},{6,7},{7,8},{8,9},{9,10},{10,1... | collective-permute-start | bytes 393224 | tf_op jit(solution)/shard_map/while/body/eval_jaxpr/ppermute | solution.py:16
  231.5 1.0 collective-permute-done
  233.1 6.2 %collective-permute-start = (bf16[32,2048]{1,0:T(8,128)(2,1)S(1)}, bf16[32,2048]{1,0:T(8,128)(2,1)S(1)}, u32[]{:S(2)}, u32[]{:S(2)}) collective-permute-start(bf16[32,2048]{1,0:T(8,128)(2,1)S(1)} %get-tuple-element.433), channel_id=1, source_target_pairs={{0,1},{1,2},{2,3},{3,4},{4,5},{5,6},{6,7},{7,8},{8,9},{9,10},{10,1... | collective-permute-start | bytes 393224 | tf_op jit(solution)/shard_map/while/body/eval_jaxpr/ppermute | solution.py:16
  241.0 6.2 %collective-permute-start = (bf16[32,2048]{1,0:T(8,128)(2,1)S(1)}, bf16[32,2048]{1,0:T(8,128)(2,1)S(1)}, u32[]{:S(2)}, u32[]{:S(2)}) collective-permute-start(bf16[32,2048]{1,0:T(8,128)(2,1)S(1)} %get-tuple-element.433), channel_id=1, source_target_pairs={{0,1},{1,2},{2,3},{3,4},{4,5},{5,6},{6,7},{7,8},{8,9},{9,10},{10,1... | collective-permute-start | bytes 393224 | tf_op jit(solution)/shard_map/while/body/eval_jaxpr/ppermute | solution.py:16
  248.9 7.6 %collective-permute-start = (bf16[32,2048]{1,0:T(8,128)(2,1)S(1)}, bf16[32,2048]{1,0:T(8,128)(2,1)S(1)}, u32[]{:S(2)}, u32[]{:S(2)}) collective-permute-start(bf16[32,2048]{1,0:T(8,128)(2,1)S(1)} %get-tuple-element.433), channel_id=1, source_target_pairs={{0,1},{1,2},{2,3},{3,4},{4,5},{5,6},{6,7},{7,8},{8,9},{9,10},{10,1... | collective-permute-start | bytes 393224 | tf_op jit(solution)/shard_map/while/body/eval_jaxpr/ppermute | solution.py:16
  256.6 1.0 collective-permute-done
  257.5 76.6 %psum.7 = f32[224]{0:T(256)S(1)} all-reduce(f32[224]{0:T(256)S(1)} %bitcast.57), channel_id=1, replica_groups=mesh['groups'=2,'tm'=16] {'tm'}, use_global_device_ids=true, to_apply=%region_9.10 | all-reduce | flops 224 | bytes 1792 | tf_op jit(solution)/shard_map/psum | solution.py:108
  (100 shorter events, 28.0 us)
Async XLA Ops:
  0.6 4.2 %collective-permute-start.1 = (f32[64,2048]{1,0:T(8,128)}, f32[64,2048]{1,0:T(8,128)S(1)}, u32[]{:S(2)}, u32[]{:S(2)}) collective-permute-start(f32[64,2048]{1,0:T(8,128)} %bitcast.54), channel_id=1, source_target_pairs={{0,1},{1,2},{2,3},{3,4},{4,5},{5,6},{6,7},{7,8},{8,9},{9,10},{10,1... | collective-permute-start | bytes 1572872 | tf_op jit(solution)/shard_map/ppermute | solution.py:16
  38.4 3.7 %collective-permute-start = (bf16[32,2048]{1,0:T(8,128)(2,1)S(1)}, bf16[32,2048]{1,0:T(8,128)(2,1)S(1)}, u32[]{:S(2)}, u32[]{:S(2)}) collective-permute-start(bf16[32,2048]{1,0:T(8,128)(2,1)S(1)} %get-tuple-element.433), channel_id=1, source_target_pairs={{0,1},{1,2},{2,3},{3,4},{4,5},{5,6},{6,7},{7,8},{8,9},{9,10},{10,1... | collective-permute-start | bytes 393224 | tf_op jit(solution)/shard_map/while/body/eval_jaxpr/ppermute | solution.py:16
  49.4 6.1 %collective-permute-start = (bf16[32,2048]{1,0:T(8,128)(2,1)S(1)}, bf16[32,2048]{1,0:T(8,128)(2,1)S(1)}, u32[]{:S(2)}, u32[]{:S(2)}) collective-permute-start(bf16[32,2048]{1,0:T(8,128)(2,1)S(1)} %get-tuple-element.433), channel_id=1, source_target_pairs={{0,1},{1,2},{2,3},{3,4},{4,5},{5,6},{6,7},{7,8},{8,9},{9,10},{10,1... | collective-permute-start | bytes 393224 | tf_op jit(solution)/shard_map/while/body/eval_jaxpr/ppermute | solution.py:16
  62.7 3.9 %collective-permute-start = (bf16[32,2048]{1,0:T(8,128)(2,1)S(1)}, bf16[32,2048]{1,0:T(8,128)(2,1)S(1)}, u32[]{:S(2)}, u32[]{:S(2)}) collective-permute-start(bf16[32,2048]{1,0:T(8,128)(2,1)S(1)} %get-tuple-element.433), channel_id=1, source_target_pairs={{0,1},{1,2},{2,3},{3,4},{4,5},{5,6},{6,7},{7,8},{8,9},{9,10},{10,1... | collective-permute-start | bytes 393224 | tf_op jit(solution)/shard_map/while/body/eval_jaxpr/ppermute | solution.py:16
  73.7 6.2 %collective-permute-start = (bf16[32,2048]{1,0:T(8,128)(2,1)S(1)}, bf16[32,2048]{1,0:T(8,128)(2,1)S(1)}, u32[]{:S(2)}, u32[]{:S(2)}) collective-permute-start(bf16[32,2048]{1,0:T(8,128)(2,1)S(1)} %get-tuple-element.433), channel_id=1, source_target_pairs={{0,1},{1,2},{2,3},{3,4},{4,5},{5,6},{6,7},{7,8},{8,9},{9,10},{10,1... | collective-permute-start | bytes 393224 | tf_op jit(solution)/shard_map/while/body/eval_jaxpr/ppermute | solution.py:16
  87.0 6.4 %collective-permute-start = (bf16[32,2048]{1,0:T(8,128)(2,1)S(1)}, bf16[32,2048]{1,0:T(8,128)(2,1)S(1)}, u32[]{:S(2)}, u32[]{:S(2)}) collective-permute-start(bf16[32,2048]{1,0:T(8,128)(2,1)S(1)} %get-tuple-element.433), channel_id=1, source_target_pairs={{0,1},{1,2},{2,3},{3,4},{4,5},{5,6},{6,7},{7,8},{8,9},{9,10},{10,1... | collective-permute-start | bytes 393224 | tf_op jit(solution)/shard_map/while/body/eval_jaxpr/ppermute | solution.py:16
  100.6 6.2 %collective-permute-start = (bf16[32,2048]{1,0:T(8,128)(2,1)S(1)}, bf16[32,2048]{1,0:T(8,128)(2,1)S(1)}, u32[]{:S(2)}, u32[]{:S(2)}) collective-permute-start(bf16[32,2048]{1,0:T(8,128)(2,1)S(1)} %get-tuple-element.433), channel_id=1, source_target_pairs={{0,1},{1,2},{2,3},{3,4},{4,5},{5,6},{6,7},{7,8},{8,9},{9,10},{10,1... | collective-permute-start | bytes 393224 | tf_op jit(solution)/shard_map/while/body/eval_jaxpr/ppermute | solution.py:16
  114.0 6.4 %collective-permute-start = (bf16[32,2048]{1,0:T(8,128)(2,1)S(1)}, bf16[32,2048]{1,0:T(8,128)(2,1)S(1)}, u32[]{:S(2)}, u32[]{:S(2)}) collective-permute-start(bf16[32,2048]{1,0:T(8,128)(2,1)S(1)} %get-tuple-element.433), channel_id=1, source_target_pairs={{0,1},{1,2},{2,3},{3,4},{4,5},{5,6},{6,7},{7,8},{8,9},{9,10},{10,1... | collective-permute-start | bytes 393224 | tf_op jit(solution)/shard_map/while/body/eval_jaxpr/ppermute | solution.py:16
  121.1 12.7 %collective-permute-start = (bf16[32,2048]{1,0:T(8,128)(2,1)S(1)}, bf16[32,2048]{1,0:T(8,128)(2,1)S(1)}, u32[]{:S(2)}, u32[]{:S(2)}) collective-permute-start(bf16[32,2048]{1,0:T(8,128)(2,1)S(1)} %get-tuple-element.433), channel_id=1, source_target_pairs={{0,1},{1,2},{2,3},{3,4},{4,5},{5,6},{6,7},{7,8},{8,9},{9,10},{10,1... | collective-permute-start | bytes 393224 | tf_op jit(solution)/shard_map/while/body/eval_jaxpr/ppermute | solution.py:16
  134.5 6.3 %collective-permute-start = (bf16[32,2048]{1,0:T(8,128)(2,1)S(1)}, bf16[32,2048]{1,0:T(8,128)(2,1)S(1)}, u32[]{:S(2)}, u32[]{:S(2)}) collective-permute-start(bf16[32,2048]{1,0:T(8,128)(2,1)S(1)} %get-tuple-element.433), channel_id=1, source_target_pairs={{0,1},{1,2},{2,3},{3,4},{4,5},{5,6},{6,7},{7,8},{8,9},{9,10},{10,1... | collective-permute-start | bytes 393224 | tf_op jit(solution)/shard_map/while/body/eval_jaxpr/ppermute | solution.py:16
  141.5 12.8 %collective-permute-start = (bf16[32,2048]{1,0:T(8,128)(2,1)S(1)}, bf16[32,2048]{1,0:T(8,128)(2,1)S(1)}, u32[]{:S(2)}, u32[]{:S(2)}) collective-permute-start(bf16[32,2048]{1,0:T(8,128)(2,1)S(1)} %get-tuple-element.433), channel_id=1, source_target_pairs={{0,1},{1,2},{2,3},{3,4},{4,5},{5,6},{6,7},{7,8},{8,9},{9,10},{10,1... | collective-permute-start | bytes 393224 | tf_op jit(solution)/shard_map/while/body/eval_jaxpr/ppermute | solution.py:16
  154.9 6.3 %collective-permute-start = (bf16[32,2048]{1,0:T(8,128)(2,1)S(1)}, bf16[32,2048]{1,0:T(8,128)(2,1)S(1)}, u32[]{:S(2)}, u32[]{:S(2)}) collective-permute-start(bf16[32,2048]{1,0:T(8,128)(2,1)S(1)} %get-tuple-element.433), channel_id=1, source_target_pairs={{0,1},{1,2},{2,3},{3,4},{4,5},{5,6},{6,7},{7,8},{8,9},{9,10},{10,1... | collective-permute-start | bytes 393224 | tf_op jit(solution)/shard_map/while/body/eval_jaxpr/ppermute | solution.py:16
  161.9 8.2 %collective-permute-start = (bf16[32,2048]{1,0:T(8,128)(2,1)S(1)}, bf16[32,2048]{1,0:T(8,128)(2,1)S(1)}, u32[]{:S(2)}, u32[]{:S(2)}) collective-permute-start(bf16[32,2048]{1,0:T(8,128)(2,1)S(1)} %get-tuple-element.433), channel_id=1, source_target_pairs={{0,1},{1,2},{2,3},{3,4},{4,5},{5,6},{6,7},{7,8},{8,9},{9,10},{10,1... | collective-permute-start | bytes 393224 | tf_op jit(solution)/shard_map/while/body/eval_jaxpr/ppermute | solution.py:16
  170.9 7.2 %collective-permute-start = (bf16[32,2048]{1,0:T(8,128)(2,1)S(1)}, bf16[32,2048]{1,0:T(8,128)(2,1)S(1)}, u32[]{:S(2)}, u32[]{:S(2)}) collective-permute-start(bf16[32,2048]{1,0:T(8,128)(2,1)S(1)} %get-tuple-element.433), channel_id=1, source_target_pairs={{0,1},{1,2},{2,3},{3,4},{4,5},{5,6},{6,7},{7,8},{8,9},{9,10},{10,1... | collective-permute-start | bytes 393224 | tf_op jit(solution)/shard_map/while/body/eval_jaxpr/ppermute | solution.py:16
  178.8 13.7 %collective-permute-start = (bf16[32,2048]{1,0:T(8,128)(2,1)S(1)}, bf16[32,2048]{1,0:T(8,128)(2,1)S(1)}, u32[]{:S(2)}, u32[]{:S(2)}) collective-permute-start(bf16[32,2048]{1,0:T(8,128)(2,1)S(1)} %get-tuple-element.433), channel_id=1, source_target_pairs={{0,1},{1,2},{2,3},{3,4},{4,5},{5,6},{6,7},{7,8},{8,9},{9,10},{10,1... | collective-permute-start | bytes 393224 | tf_op jit(solution)/shard_map/while/body/eval_jaxpr/ppermute | solution.py:16
  193.2 7.2 %collective-permute-start = (bf16[32,2048]{1,0:T(8,128)(2,1)S(1)}, bf16[32,2048]{1,0:T(8,128)(2,1)S(1)}, u32[]{:S(2)}, u32[]{:S(2)}) collective-permute-start(bf16[32,2048]{1,0:T(8,128)(2,1)S(1)} %get-tuple-element.433), channel_id=1, source_target_pairs={{0,1},{1,2},{2,3},{3,4},{4,5},{5,6},{6,7},{7,8},{8,9},{9,10},{10,1... | collective-permute-start | bytes 393224 | tf_op jit(solution)/shard_map/while/body/eval_jaxpr/ppermute | solution.py:16
  201.1 7.2 %collective-permute-start = (bf16[32,2048]{1,0:T(8,128)(2,1)S(1)}, bf16[32,2048]{1,0:T(8,128)(2,1)S(1)}, u32[]{:S(2)}, u32[]{:S(2)}) collective-permute-start(bf16[32,2048]{1,0:T(8,128)(2,1)S(1)} %get-tuple-element.433), channel_id=1, source_target_pairs={{0,1},{1,2},{2,3},{3,4},{4,5},{5,6},{6,7},{7,8},{8,9},{9,10},{10,1... | collective-permute-start | bytes 393224 | tf_op jit(solution)/shard_map/while/body/eval_jaxpr/ppermute | solution.py:16
  209.0 7.2 %collective-permute-start = (bf16[32,2048]{1,0:T(8,128)(2,1)S(1)}, bf16[32,2048]{1,0:T(8,128)(2,1)S(1)}, u32[]{:S(2)}, u32[]{:S(2)}) collective-permute-start(bf16[32,2048]{1,0:T(8,128)(2,1)S(1)} %get-tuple-element.433), channel_id=1, source_target_pairs={{0,1},{1,2},{2,3},{3,4},{4,5},{5,6},{6,7},{7,8},{8,9},{9,10},{10,1... | collective-permute-start | bytes 393224 | tf_op jit(solution)/shard_map/while/body/eval_jaxpr/ppermute | solution.py:16
  216.9 7.6 %collective-permute-start = (bf16[32,2048]{1,0:T(8,128)(2,1)S(1)}, bf16[32,2048]{1,0:T(8,128)(2,1)S(1)}, u32[]{:S(2)}, u32[]{:S(2)}) collective-permute-start(bf16[32,2048]{1,0:T(8,128)(2,1)S(1)} %get-tuple-element.433), channel_id=1, source_target_pairs={{0,1},{1,2},{2,3},{3,4},{4,5},{5,6},{6,7},{7,8},{8,9},{9,10},{10,1... | collective-permute-start | bytes 393224 | tf_op jit(solution)/shard_map/while/body/eval_jaxpr/ppermute | solution.py:16
  225.2 7.2 %collective-permute-start = (bf16[32,2048]{1,0:T(8,128)(2,1)S(1)}, bf16[32,2048]{1,0:T(8,128)(2,1)S(1)}, u32[]{:S(2)}, u32[]{:S(2)}) collective-permute-start(bf16[32,2048]{1,0:T(8,128)(2,1)S(1)} %get-tuple-element.433), channel_id=1, source_target_pairs={{0,1},{1,2},{2,3},{3,4},{4,5},{5,6},{6,7},{7,8},{8,9},{9,10},{10,1... | collective-permute-start | bytes 393224 | tf_op jit(solution)/shard_map/while/body/eval_jaxpr/ppermute | solution.py:16
  233.1 7.2 %collective-permute-start = (bf16[32,2048]{1,0:T(8,128)(2,1)S(1)}, bf16[32,2048]{1,0:T(8,128)(2,1)S(1)}, u32[]{:S(2)}, u32[]{:S(2)}) collective-permute-start(bf16[32,2048]{1,0:T(8,128)(2,1)S(1)} %get-tuple-element.433), channel_id=1, source_target_pairs={{0,1},{1,2},{2,3},{3,4},{4,5},{5,6},{6,7},{7,8},{8,9},{9,10},{10,1... | collective-permute-start | bytes 393224 | tf_op jit(solution)/shard_map/while/body/eval_jaxpr/ppermute | solution.py:16
  241.0 7.2 %collective-permute-start = (bf16[32,2048]{1,0:T(8,128)(2,1)S(1)}, bf16[32,2048]{1,0:T(8,128)(2,1)S(1)}, u32[]{:S(2)}, u32[]{:S(2)}) collective-permute-start(bf16[32,2048]{1,0:T(8,128)(2,1)S(1)} %get-tuple-element.433), channel_id=1, source_target_pairs={{0,1},{1,2},{2,3},{3,4},{4,5},{5,6},{6,7},{7,8},{8,9},{9,10},{10,1... | collective-permute-start | bytes 393224 | tf_op jit(solution)/shard_map/while/body/eval_jaxpr/ppermute | solution.py:16
  248.9 8.6 %collective-permute-start = (bf16[32,2048]{1,0:T(8,128)(2,1)S(1)}, bf16[32,2048]{1,0:T(8,128)(2,1)S(1)}, u32[]{:S(2)}, u32[]{:S(2)}) collective-permute-start(bf16[32,2048]{1,0:T(8,128)(2,1)S(1)} %get-tuple-element.433), channel_id=1, source_target_pairs={{0,1},{1,2},{2,3},{3,4},{4,5},{5,6},{6,7},{7,8},{8,9},{9,10},{10,1... | collective-permute-start | bytes 393224 | tf_op jit(solution)/shard_map/while/body/eval_jaxpr/ppermute | solution.py:16
  257.5 77.2 %copy-start = (f32[1,224,2048]{2,1,0:T(8,128)}, f32[1,224,2048]{2,1,0:T(8,128)S(1)}, u32[]{:S(2)}) copy-start(f32[1,224,2048]{2,1,0:T(8,128)S(1)} %get-tuple-element.273) | copy-start | bytes 5505028
where the time goes:
time: 336 us; the launch traced here: 335 us
  starting transfers between devices  146 us (43%)
  blocking collectives  76.6 us (23%)
  matrix products  61.3 us (18%)
  other arithmetic  24.4 us (7%)
  waiting for transfers between devices  21.1 us (6%)
    ppermute x23, starting transfers between devices, shifted(): lax.ppermute(value, axis, [(source, source + steps) for source in range(i...  146 us
    psum x1, blocking collectives, per_device(): log_scale = lax.psum(local_log, 'tm') / (tm_count * local_slices - 1)  76.6 us
    dot_general x7, matrix products, push_forward(): jnp.dot(weighted, kernel, preferred_element_type=jnp.float32)  35.2 us
    dot_general x4, matrix products, one_block(): lax.dot_general(segment, target, (((0,), (0,)), ((), ())), precision=lax....  26.1 us
    ppermute x23, waiting for transfers between devices, shifted(): lax.ppermute(value, axis, [(source, source + steps) for source in range(i...  21.1 us
    convert_element_type x22, other arithmetic, per_device(): (jnp.arange(point_count, dtype=jnp.int32)[None, :] < supports[:, None]).a...  14.4 us
    convert_element_type x7, other arithmetic, section(): outgoing = (message * block_pot[local_slices - 1]).astype(jnp.bfloat16)  7.46 us
  transfers between devices with their start and end apart: 23, of which 22 were waited for; matrix products, arithmetic and copies ran while one was open for 0% of the time, Pallas kernels for 0%

commit v1 on v0

v1 whole, which is shorter than its diff:
```python
import functools
import math

import jax
import jax.numpy as jnp
from jax import lax
from jax.experimental import pallas as pl
from jax.experimental.pallas import tpu as pltpu
from jax.sharding import PartitionSpec as P

A_DECAY = 0.8
EPS_SCALE = 0.05
MESH = pl.DeviceIdType.MESH
F32 = jnp.float32
BF16 = jnp.bfloat16

TEAM = 4
ROWS = 64

R_PT, R_PRED, R_POT, R_G, R_W, R_LW, R_GA, R_LG, R_FIN = 0, 4, 5, 9, 13, 14, 15, 17, 21
N_RECV = 22
S_PT, S_PRED, S_POT, S_G, S_W, S_LW, S_GA, S_LG, S_W1, S_L1, S_FIN = 0, 3, 4, 7, 11, 12, 13, 16, 17, 20, 23


def split2(v):
    hi = v.astype(BF16)
    lo = (v - hi.astype(F32)).astype(BF16)
    return hi, lo


def split3(v):
    hi = v.astype(BF16)
    rest = v - hi.astype(F32)
    mid, lo = split2(rest)
    return hi.astype(F32), mid.astype(F32), lo.astype(F32)


def kernel(n_tm, starts, half, pts_in, pot_in, sup_in, out, logout,
           pts, pts2, potb, potb2, potr, kern, kern2, opa, opb, wbuf, w1, gat, gat2,
           push, logacc, log1, loggat, logfin, ssem, rsem):
    dim = pts_in.shape[1]
    cols = pot_in.shape[1]
    me = lax.axis_index("tm")
    q = lax.rem(me, TEAM)
    g = lax.div(me, TEAM)
    base = me - q
    n_g = n_tm // TEAM
    last = n_tm - 1
    sib = base + q + 1 - 2 * lax.rem(q, 2)
    yq = lax.rem(q + 2, TEAM)
    ymate = base + yq
    is_first = g == 0
    is_last = g == n_g - 1
    inner = jnp.logical_not(is_first)

    def rc(src, dst, s, r, dev):
        return pltpu.make_async_remote_copy(
            src_ref=src, dst_ref=dst, send_sem=ssem.at[s], recv_sem=rsem.at[r],
            device_id={"tm": dev}, device_id_type=MESH)

    def greet(dev):
        pl.semaphore_signal(barrier, inc=1, device_id={"tm": dev}, device_id_type=MESH)

    barrier = pltpu.get_barrier_semaphore()
    for d in range(1, TEAM):
        greet(base + lax.rem(q + d, TEAM))

    @pl.when(inner)
    def _():
        greet(me - TEAM)

    @pl.when(jnp.logical_not(is_last))
    def _():
        greet(me + TEAM)

    @pl.when(me != last)
    def _():
        greet(last)

    @pl.when(me == last)
    def _():
        for dev in range(n_tm - 1):
            greet(dev)

    support = sup_in[0]
    lane = lax.broadcasted_iota(jnp.int32, (8, half), 1)
    pts[q, 0:dim, :] = pts_in[0, :, 0:half]
    pts[q, dim:dim + 8, :] = (lane < support).astype(F32)
    pts2[0:dim, :] = pts_in[0, :, half:2 * half]
    pts2[dim:dim + 8, :] = (lane + half < support).astype(F32)
    for b in range(TEAM):
        potb[b] = pot_in[0, starts[b]:starts[b] + ROWS, 0:half].astype(BF16)

    @pl.when(me == 0)
    def _():
        for b in range(TEAM):
            potb2[b] = pot_in[0, starts[b]:starts[b] + ROWS, half:2 * half].astype(BF16)

    peers = (TEAM - 1 + jnp.where(is_first, 0, 1) + jnp.where(is_last, 0, 1)
             + jnp.where(me == last, n_tm - 1, 1))
    pl.semaphore_wait(barrier, peers)

    to_sib = rc(pts.at[q], pts.at[q], S_PT, R_PT + q, sib)
    to_ymate = rc(pts.at[q], pts.at[q], S_PT + 1, R_PT + q, ymate)
    to_sib.start()
    head = [rc(pts2, pts.at[TEAM], S_GA + 2, R_PRED, 1),
            rc(potb, gat, S_GA, R_GA, 1),
            rc(potb2, gat2, S_GA + 1, R_GA + 1, 1)]

    @pl.when(me == 0)
    def _():
        for c in head:
            c.start()

    to_ymate.start()
    sends_pot = jnp.logical_or(inner, q >= 2)
    pot_copies = []
    for d in range(1, TEAM):
        mq = lax.rem(q + d, TEAM)
        pot_copies.append(rc(potb.at[mq], potr.at[q], S_POT + d - 1, R_POT + q, base + mq))

    @pl.when(sends_pot)
    def _():
        for c in pot_copies:
            c.start()

    potr[q] = potb[q]

    def recv_points(slot):
        rc(pts.at[slot], pts.at[slot], S_PT, R_PT + slot, me).wait_recv()

    unit = math.log2(math.e) / (2.0 * EPS_SCALE * dim)

    def generate(src, dst, res):
        x = src[0:dim, :]
        y = dst[0:dim, :]
        live = dst[dim:dim + 1, :]
        u = (-unit * A_DECAY * A_DECAY) * jnp.sum(x * x, axis=0, keepdims=True)
        v = -unit * jnp.sum(y * y, axis=0, keepdims=True)
        v = jnp.where(live > 0.0, v, -1e9)
        row = lax.broadcasted_iota(jnp.int32, (dim, half), 0)
        uh, um, ul = split3(u)
        vh, vm, vl = split3(v)
        one = jnp.where(row < 6, 1.0, 0.0)
        xh, xl = split2(x)
        yh, yl = split2(y * (2.0 * A_DECAY * unit))
        opa[0:dim, :] = xh
        opa[dim:2 * dim, :] = xh
        opa[2 * dim:3 * dim, :] = xl
        opa[3 * dim:4 * dim, :] = jnp.where(
            row == 3, uh, jnp.where(row == 4, um, jnp.where(row == 5, ul, one))).astype(BF16)
        opb[0:dim, :] = yh
        opb[dim:2 * dim, :] = yl
        opb[2 * dim:3 * dim, :] = yh
        opb[3 * dim:4 * dim, :] = jnp.where(
            row == 0, vh, jnp.where(row == 1, vm, jnp.where(row == 2, vl, one))).astype(BF16)
        tile = 256

        @pl.loop(0, half // tile)
        def _(i):
            at = pl.ds(pl.multiple_of(i * tile, tile), tile)
            e = lax.dot_general(opa[:, at], opb[...], (((0,), (0,)), ((), ())),
                                preferred_element_type=F32)
            res[at, :] = jnp.exp2(e).astype(BF16)

    def log_row(value):
        spread = jnp.broadcast_to(value, (ROWS, 128))
        r0 = lax.broadcasted_iota(jnp.int32, (ROWS, 128), 0)
        r1 = lax.broadcasted_iota(jnp.int32, (ROWS, 128), 1)
        return jnp.sum(jnp.where(r0 == r1, spread, 0.0), axis=0, keepdims=True)

    def count(ref):
        return jnp.sum(ref[dim:dim + 1, :], axis=1, keepdims=True)

    def blocks(ref):
        return ref[...].reshape(TEAM * ROWS, half)

    w1_copies = []
    for d in range(1, TEAM):
        mq = lax.rem(1 + d, TEAM)
        w1_copies.append((rc(w1.at[mq], wbuf.at[2], S_W1 + d - 1, R_W, mq),
                          rc(log1.at[mq], logacc, S_L1 + d - 1, R_LW, mq)))

    recv_points(lax.rem(sib, TEAM))

    @pl.when(me == 1)
    def _():
        head[0].wait_recv()
        generate(pts.at[0], pts.at[1], kern.at[1])
        generate(pts.at[TEAM], pts.at[1], kern.at[0])
        head[1].wait_recv()
        head[2].wait_recv()
        pushed = (jnp.dot(blocks(gat), kern[1], preferred_element_type=F32)
                  + jnp.dot(blocks(gat2), kern[0], preferred_element_type=F32))
        cs = jnp.sum(pushed, axis=1, keepdims=True)
        cnt = count(pts.at[1])
        push[:, 0:half] = pushed * (cnt / cs)
        for b in (2, 3, 0, 1):
            rows = slice(starts[b], starts[b] + ROWS)
            m = push[b * ROWS:(b + 1) * ROWS, 0:half]
            w = (m * pot_in[0, rows, 0:half]).astype(BF16)
            if b == 1:
                wbuf[2] = w
            else:
                w1[b] = w
                w1_copies[(b + 2) % TEAM][0].start()
        for b in range(TEAM):
            lr = log_row(jnp.log(cs[b * ROWS:(b + 1) * ROWS] / cnt))
            if b == 1:
                logacc[...] = jnp.broadcast_to(lr, logacc.shape)
            else:
                log1[b] = jnp.broadcast_to(lr, logacc.shape)
                w1_copies[(b + 2) % TEAM][1].start()
        for b in range(TEAM):
            out[0, starts[b]:starts[b] + ROWS, 0:half] = push[b * ROWS:(b + 1) * ROWS, 0:half]

    recv_points(yq)
    forward = rc(pts.at[yq], pts.at[yq], S_PT + 2, R_PT + yq, sib)
    forward.start()
    recv_points(lax.rem(lax.rem(sib, TEAM) + 2, TEAM))
    pred = rc(pts.at[TEAM - 1], pts.at[TEAM], S_PRED, R_PRED, me + TEAM)

    @pl.when(jnp.logical_not(is_last))
    def _():
        pred.start()

    generate(pts.at[1], pts.at[2], kern.at[2])

    @pl.when(jnp.logical_or(jnp.logical_not(is_last), q == TEAM - 1))
    def _():
        generate(pts.at[2], pts.at[3], kern.at[3])

    @pl.when(me == last)
    def _():
        generate(pts.at[2], pts2, kern2)

    @pl.when(inner)
    def _():
        generate(pts.at[0], pts.at[1], kern.at[1])
        pred.wait_recv()
        generate(pts.at[TEAM], pts.at[0], kern.at[0])

    w_in = rc(wbuf.at[TEAM], wbuf.at[0], S_W, R_W, me + TEAM)
    l_in = rc(logacc, logacc, S_LW, R_LW, me + TEAM)

    @pl.when(me != 1)
    def _():
        w_in.wait_recv()
        l_in.wait_recv()

    to_owner = [rc(wbuf.at[s], gat.at[q], S_G + s, R_G + q, base + s) for s in range(TEAM)]

    def offer(s):
        @pl.when(q == s)
        def _():
            gat[q] = wbuf[s]

        @pl.when(q != s)
        def _():
            to_owner[s].start()

    def step(s):
        offer(s)
        pushed = jnp.dot(wbuf[s], kern[s], preferred_element_type=F32)
        cs = jnp.sum(pushed, axis=1, keepdims=True)
        cnt = count(pts.at[s])

        @pl.when(q != s)
        def _():
            rc(potr.at[s], potr.at[s], S_POT, R_POT + s, me).wait_recv()

        wbuf[s + 1] = (pushed * (cnt / cs) * potr[s].astype(F32)).astype(BF16)
        if s == TEAM - 1:
            w_in.start()
        logacc[...] += jnp.broadcast_to(log_row(jnp.log(cs / cnt)), logacc.shape)

    @pl.when(inner)
    def _():
        step(0)
        step(1)

    step(2)

    l_gat = rc(logacc, loggat.at[q], S_LG, R_LG + q, last)

    @pl.when(jnp.logical_not(is_last))
    def _():
        step(3)
        l_in.start()

    @pl.when(is_last)
    def _():
        offer(3)

        @pl.when(me != last)
        def _():
            l_gat.start()
            rc(potr.at[3], potr.at[3], S_POT, R_POT + 3, me).wait_recv()

        @pl.when(me == last)
        def _():
            loggat[q] = logacc[...]

    @pl.when(jnp.logical_or(inner, q >= 2))
    def _():
        for d in range(1, TEAM):
            mq = lax.rem(q + d, TEAM)
            rc(gat.at[mq], gat.at[mq], S_G, R_G + mq, me).wait_recv()

    @pl.when(me == 0)
    def _():
        full = lax.broadcasted_iota(jnp.int32, (cols, 2 * half), 1)
        out[0] = (full < support).astype(F32)

    @pl.when(jnp.logical_and(me != 0, me != last))
    def _():
        out[0, :, half:2 * half] = jnp.zeros((cols, half), F32)

    @pl.when(jnp.logical_and(jnp.logical_or(inner, q >= 2), me != last))
    def _():
        pushed = jnp.dot(blocks(gat), kern[q], preferred_element_type=F32)
        cs = jnp.sum(pushed, axis=1, keepdims=True)
        push[:, 0:half] = pushed * (count(pts.at[q]) / cs)
        for b in range(TEAM):
            out[0, starts[b]:starts[b] + ROWS, 0:half] = push[b * ROWS:(b + 1) * ROWS, 0:half]

    fin = [rc(logfin, logfin, S_FIN + dev, R_FIN, dev) for dev in range(n_tm - 1)]

    @pl.when(me == last)
    def _():
        pa = jnp.dot(blocks(gat), kern[TEAM - 1], preferred_element_type=F32)
        pb = jnp.dot(blocks(gat), kern2[...], preferred_element_type=F32)
        cs = jnp.sum(pa, axis=1, keepdims=True) + jnp.sum(pb, axis=1, keepdims=True)
        cnt = count(pts.at[TEAM - 1]) + count(pts2)
        term = jnp.log(cs / cnt)
        for b in range(TEAM - 1):
            rc(loggat.at[b], loggat.at[b], S_LG, R_LG + b, me).wait_recv()
        logfin[...] = jnp.zeros_like(logfin)
        for b in range(TEAM):
            total = loggat[b, 0:1, :] + log_row(term[b * ROWS:(b + 1) * ROWS])
            logfin[b:b + 1, :] = total * (1.0 / (n_tm - 1))
        for c in fin:
            c.start()
        push[:, 0:half] = pa * (cnt / cs)
        push[:, half:2 * half] = pb * (cnt / cs)
        for b in range(TEAM):
            out[0, starts[b]:starts[b] + ROWS, :] = push[b * ROWS:(b + 1) * ROWS, :]
        for c in fin:
            c.wait_send()

    to_sib.wait_send()
    to_ymate.wait_send()
    forward.wait_send()

    @pl.when(me == 0)
    def _():
        for c in head:
            c.wait_send()

    @pl.when(me == 1)
    def _():
        for a, b in w1_copies:
            a.wait_send()
            b.wait_send()

    @pl.when(sends_pot)
    def _():
        for c in pot_copies:
            c.wait_send()

    @pl.when(jnp.logical_not(is_last))
    def _():
        pred.wait_send()
        w_in.wait_send()
        l_in.wait_send()

    for s in range(TEAM):
        sent = jnp.logical_and(q != s, jnp.logical_or(inner, s >= 2))

        @pl.when(sent)
        def _(s=s):
            to_owner[s].wait_send()

    @pl.when(jnp.logical_and(is_last, me != last))
    def _():
        l_gat.wait_send()

    @pl.when(me != last)
    def _():
        rc(logfin, logfin, S_FIN, R_FIN, me).wait_recv()

    logout[...] = logfin[...]


def per_device(n_tm, points, potentials, supports):
    slices, dim, count = points.shape
    cols = potentials.shape[1]
    half = count // 2
    starts = [(b * (cols - ROWS) // (TEAM - 1)) // 16 * 16 for b in range(TEAM)]
    vm = lambda shape, dtype: pltpu.VMEM(shape, dtype)
    messages, logs = pl.pallas_call(
        functools.partial(kernel, n_tm, starts, half),
        out_shape=(jax.ShapeDtypeStruct((slices, cols, count), F32),
                   jax.ShapeDtypeStruct((8, 128), F32)),
        in_specs=[pl.BlockSpec(memory_space=pltpu.VMEM),
                  pl.BlockSpec(memory_space=pltpu.VMEM),
                  pl.BlockSpec(memory_space=pltpu.SMEM)],
        out_specs=(pl.BlockSpec(memory_space=pltpu.VMEM),
                   pl.BlockSpec(memory_space=pltpu.VMEM)),
        scratch_shapes=[
            vm((TEAM + 1, dim + 8, half), F32),
            vm((dim + 8, half), F32),
            vm((TEAM, ROWS, half), BF16),
            vm((TEAM, ROWS, half), BF16),
            vm((TEAM, ROWS, half), BF16),
            vm((TEAM, half, half), BF16),
            vm((half, half), BF16),
            vm((4 * dim, half), BF16),
            vm((4 * dim, half), BF16),
            vm((TEAM + 1, ROWS, half), BF16),
            vm((TEAM, ROWS, half), BF16),
            vm((TEAM, ROWS, half), BF16),
            vm((TEAM, ROWS, half), BF16),
            vm((TEAM * ROWS, 2 * half), F32),
            vm((8, 128), F32),
            vm((TEAM, 8, 128), F32),
            vm((TEAM, 8, 128), F32),
            vm((8, 128), F32),
            pltpu.SemaphoreType.DMA((S_FIN + n_tm,)),
            pltpu.SemaphoreType.DMA((N_RECV,)),
        ],
        compiler_params=pltpu.CompilerParams(
            collective_id=0, has_side_effects=True, vmem_limit_bytes=48 * 1024 * 1024),
    )(points, potentials, supports)
    ends = starts[1:] + [cols]
    log_scale = jnp.concatenate(
        [logs[b, 0:ends[b] - starts[b]] for b in range(TEAM)])
    return messages, log_scale


def solution(mesh):
    placed = (P(("groups", "tm"), None, None), P(("groups", "tm"), None, None), P(("groups", "tm")))
    return jax.shard_map(
        functools.partial(per_device, mesh.shape["tm"]),
        mesh=mesh,
        in_specs=placed,
        out_specs=(P(("groups", "tm"), None, None), P("groups")),
        check_vma=False,
    )
```

time: 336 us -> 58.9 us (0.18)
  starting transfers between devices: 146 us -> 0 us
  blocking collectives: 76.6 us -> 0 us
  matrix products: 61.3 us -> 0 us
  Pallas kernels: 0 us -> 53 us
  other arithmetic: 24.4 us -> 0.64 us
  waiting for transfers between devices: 21.1 us -> 0 us
    ppermute x23 -> x0, starting transfers between devices: 146 us -> none  [shifted(): lax.ppermute(value, axis, [(source, source + steps) for source in range(i...]
    psum x1 -> x0, blocking collectives: 76.6 us -> none  [per_device(): log_scale = lax.psum(local_log, 'tm') / (tm_count * local_slices - 1)]
    dot_general x11 -> x0, matrix products: 61.3 us -> none  [the longest x7 35.2 us: push_forward(): jnp.dot(weighted, kernel, preferred_element_type=jnp.float32)]
    pallas_call x0 -> x1, Pallas kernels: none -> 53 us  [per_device(): pl.pallas_call(functools.partial(kernel, n_tm, starts, half), out_shape=(...]
    convert_element_type x29 -> x0, other arithmetic: 21.9 us -> none  [the longest x22 14.4 us: per_device(): (jnp.arange(point_count, dtype=jnp.int32)[None, :] < supports[:, None]).a...]
    ppermute x23 -> x0, waiting for transfers between devices: 21.1 us -> none  [shifted(): lax.ppermute(value, axis, [(source, source + steps) for source in range(i...]
    unnamed x2 -> x5, local copies, waits for them, and re-layouts: 0.01 us -> 3.76 us
  transfers between devices with their start and end apart: 23 -> 0, of which waited for: 22 -> 0; matrix products, arithmetic and copies ran while one was open for 0% -> 0% of each run, Pallas kernels for 0% -> 0%
where the time goes in v1:
time: 58.9 us; the launch traced here: 58.7 us
  Pallas kernels  53 us (90%)
  local copies, waits for them, and re-layouts  3.77 us (6%)
  between operations  1.31 us (2%)
  other arithmetic  0.64 us (1%)
    pallas_call x1, Pallas kernels, per_device(): pl.pallas_call(functools.partial(kernel, n_tm, starts, half), out_shape=(...  53 us
    unnamed x5, local copies, waits for them, and re-layouts  3.76 us

profile of v1, /device:TPU:0, one launch (start us, length us, event | category | flops | bytes accessed | tf_op | source)
XLA Modules:
  0.0 58.7 jit_solution(59788301503792495)
XLA Ops:
  1.3 0.0 copy-start
  1.3 1.5 %copy-done = f32[1,224,2048]{2,1,0:T(8,128)S(1)} copy-done((f32[1,224,2048]{2,1,0:T(8,128)S(1)}, f32[1,224,2048]{2,1,0:T(8,128)}, u32[]{:S(2)}) %copy-start) | copy-done | bytes 1835032
  2.8 0.0 copy-start.1
  2.8 1.0 %copy-done.1 = f32[1,64,2048]{2,1,0:T(8,128)S(1)} copy-done((f32[1,64,2048]{2,1,0:T(8,128)S(1)}, f32[1,64,2048]{2,1,0:T(8,128)}, u32[]{:S(2)}) %copy-start.1) | copy-done | bytes 524312
  3.8 53.0 %shard_map.50 = (f32[1,224,2048]{2,1,0:T(8,128)S(1)}, f32[8,128]{1,0:T(8,128)S(1)}) custom-call(f32[1,64,2048]{2,1,0:T(8,128)S(1)} %copy-done.1, f32[1,224,2048]{2,1,0:T(8,128)S(1)} %copy-done, s32[1]{0:T(128)S(6)} %copy.6.sup_in), custom_call_target="tpu_custom_call" | custom-call | tf_op jit(solution)/shard_map/pallas_call | solution.py:401
  56.8 0.6 %pad_maximum_fusion = f32[224]{0:T(256)} fusion(f32[64]{0:T(128)S(1)} %get-tuple-element.9, f32[64]{0:T(128)S(1)} %get-tuple-element.8, f32[48]{0:T(128)S(1)} %get-tuple-element.7, f32[48]{0:T(128)S(1)} %get-tuple-element.6), kind=kLoop, calls=%fused_computation | loop fusion | flops 672 | bytes 1792 | tf_op jit(solution)/shard_map/concatenate | solution.py:436
  57.5 1.2 %copy.7 = f32[1,224,2048]{2,1,0:T(8,128)} copy(f32[1,224,2048]{2,1,0:T(8,128)S(1)} %get-tuple-element.12) | data formatting | bytes 3670016
  (2 shorter events, 0.0 us)
Async XLA Ops:
  1.3 1.5 %copy-start = (f32[1,224,2048]{2,1,0:T(8,128)S(1)}, f32[1,224,2048]{2,1,0:T(8,128)}, u32[]{:S(2)}) copy-start(f32[1,224,2048]{2,1,0:T(8,128)} %pot_in.1) | copy-start | bytes 5505028
  2.8 1.0 %copy-start.1 = (f32[1,64,2048]{2,1,0:T(8,128)S(1)}, f32[1,64,2048]{2,1,0:T(8,128)}, u32[]{:S(2)}) copy-start(f32[1,64,2048]{2,1,0:T(8,128)} %pts_in.1) | copy-start | bytes 1572868

commit v2 on v1

--- a/solution.py
+++ b/solution.py
@@ -35,11 +35,11 @@
     return hi.astype(F32), mid.astype(F32), lo.astype(F32)
 
 
-def kernel(n_tm, starts, half, pts_in, pot_in, sup_in, out, logout,
+def kernel(n_tm, starts, half, pts_hbm, pot_hbm, sup_in, out, logout,
            pts, pts2, potb, potb2, potr, kern, kern2, opa, opb, wbuf, w1, gat, gat2,
-           push, logacc, log1, loggat, logfin, ssem, rsem):
-    dim = pts_in.shape[1]
-    cols = pot_in.shape[1]
+           push, logacc, log1, loggat, logfin, pot_in, ssem, rsem, lsem):
+    dim = pts_hbm.shape[1]
+    cols = pot_hbm.shape[1]
     me = lax.axis_index("tm")
     q = lax.rem(me, TEAM)
     g = lax.div(me, TEAM)
@@ -84,18 +84,15 @@
 
     support = sup_in[0]
     lane = lax.broadcasted_iota(jnp.int32, (8, half), 1)
-    pts[q, 0:dim, :] = pts_in[0, :, 0:half]
+    loads = [pltpu.make_async_copy(pts_hbm.at[0, :, 0:half], pts.at[q, 0:dim], lsem.at[0]),
+             pltpu.make_async_copy(pts_hbm.at[0, :, half:2 * half], pts2.at[0:dim], lsem.at[1]),
+             pltpu.make_async_copy(pot_hbm, pot_in, lsem.at[2])]
+    for c in loads:
+        c.start()
     pts[q, dim:dim + 8, :] = (lane < support).astype(F32)
-    pts2[0:dim, :] = pts_in[0, :, half:2 * half]
     pts2[dim:dim + 8, :] = (lane + half < support).astype(F32)
-    for b in range(TEAM):
-        potb[b] = pot_in[0, starts[b]:starts[b] + ROWS, 0:half].astype(BF16)
-
-    @pl.when(me == 0)
-    def _():
-        for b in range(TEAM):
-            potb2[b] = pot_in[0, starts[b]:starts[b] + ROWS, half:2 * half].astype(BF16)
-
+    loads[0].wait()
+    loads[1].wait()
     peers = (TEAM - 1 + jnp.where(is_first, 0, 1) + jnp.where(is_last, 0, 1)
              + jnp.where(me == last, n_tm - 1, 1))
     pl.semaphore_wait(barrier, peers)
@@ -109,10 +106,26 @@
 
     @pl.when(me == 0)
     def _():
-        for c in head:
-            c.start()
-
-    to_ymate.start()
+        head[0].start()
+
+    @pl.when(me != 0)
+    def _():
+        to_ymate.start()
+
+    loads[2].wait()
+    for b in range(TEAM):
+        potb[b] = pot_in[0, starts[b]:starts[b] + ROWS, 0:half].astype(BF16)
+
+    @pl.when(me == 0)
+    def _():
+        for b in range(TEAM):
+            potb2[b] = pot_in[0, starts[b]:starts[b] + ROWS, half:2 * half].astype(BF16)
+
+    @pl.when(me == 0)
+    def _():
+        head[1].start()
+        head[2].start()
+
     sends_pot = jnp.logical_or(inner, q >= 2)
     pot_copies = []
     for d in range(1, TEAM):
@@ -214,10 +227,18 @@
         for b in range(TEAM):
             out[0, starts[b]:starts[b] + ROWS, 0:half] = push[b * ROWS:(b + 1) * ROWS, 0:half]
 
-    recv_points(yq)
     forward = rc(pts.at[yq], pts.at[yq], S_PT + 2, R_PT + yq, sib)
-    forward.start()
-    recv_points(lax.rem(lax.rem(sib, TEAM) + 2, TEAM))
+    diag = lax.rem(lax.rem(sib, TEAM) + 2, TEAM)
+
+    @pl.when(me != 2)
+    def _():
+        recv_points(yq)
+        forward.start()
+
+    @pl.when(me != 3)
+    def _():
+        recv_points(diag)
+
     pred = rc(pts.at[TEAM - 1], pts.at[TEAM], S_PRED, R_PRED, me + TEAM)
 
     @pl.when(jnp.logical_not(is_last))
@@ -260,7 +281,13 @@
             to_owner[s].start()
 
     def step(s):
-        offer(s)
+        if s == 2:
+            @pl.when(jnp.logical_not(is_last))
+            def _():
+                offer(s)
+        else:
+            offer(s)
+
         pushed = jnp.dot(wbuf[s], kern[s], preferred_element_type=F32)
         cs = jnp.sum(pushed, axis=1, keepdims=True)
         cnt = count(pts.at[s])
@@ -295,6 +322,12 @@
         @pl.when(me != last)
         def _():
             l_gat.start()
+            to_owner[3].wait_send()
+
+        offer(2)
+
+        @pl.when(me != last)
+        def _():
             rc(potr.at[3], potr.at[3], S_POT, R_POT + 3, me).wait_recv()
 
         @pl.when(me == last)
@@ -349,8 +382,14 @@
             c.wait_send()
 
     to_sib.wait_send()
-    to_ymate.wait_send()
-    forward.wait_send()
+
+    @pl.when(me != 0)
+    def _():
+        to_ymate.wait_send()
+
+    @pl.when(me != 2)
+    def _():
+        forward.wait_send()
 
     @pl.when(me == 0)
     def _():
@@ -376,6 +415,8 @@
 
     for s in range(TEAM):
         sent = jnp.logical_and(q != s, jnp.logical_or(inner, s >= 2))
+        if s == 3:
+            sent = jnp.logical_and(sent, jnp.logical_not(is_last))
 
         @pl.when(sent)
         def _(s=s):
@@ -402,8 +443,8 @@
         functools.partial(kernel, n_tm, starts, half),
         out_shape=(jax.ShapeDtypeStruct((slices, cols, count), F32),
                    jax.ShapeDtypeStruct((8, 128), F32)),
-        in_specs=[pl.BlockSpec(memory_space=pltpu.VMEM),
-                  pl.BlockSpec(memory_space=pltpu.VMEM),
+        in_specs=[pl.BlockSpec(memory_space=pltpu.HBM),
+                  pl.BlockSpec(memory_space=pltpu.HBM),
                   pl.BlockSpec(memory_space=pltpu.SMEM)],
         out_specs=(pl.BlockSpec(memory_space=pltpu.VMEM),
                    pl.BlockSpec(memory_space=pltpu.VMEM)),
@@ -426,8 +467,10 @@
             vm((TEAM, 8, 128), F32),
             vm((TEAM, 8, 128), F32),
             vm((8, 128), F32),
+            vm((slices, cols, count), F32),
             pltpu.SemaphoreType.DMA((S_FIN + n_tm,)),
             pltpu.SemaphoreType.DMA((N_RECV,)),
+            pltpu.SemaphoreType.DMA((3,)),
         ],
         compiler_params=pltpu.CompilerParams(
             collective_id=0, has_side_effects=True, vmem_limit_bytes=48 * 1024 * 1024),

time: 58.9 us -> 58.5 us (level)
  no operation moved by 1% of the time
where the time goes in v2:
time: 58.5 us; the launch traced here: 58.3 us
  Pallas kernels  52.6 us (90%)
  local copies, waits for them, and re-layouts  3.77 us (6%)
  between operations  1.31 us (2%)
  other arithmetic  0.64 us (1%)
    pallas_call x1, Pallas kernels, per_device(): pl.pallas_call(functools.partial(kernel, n_tm, starts, half), out_shape=(...  52.6 us
    unnamed x5, local copies, waits for them, and re-layouts  3.76 us

profile of v2, /device:TPU:0, one launch (start us, length us, event | category | flops | bytes accessed | tf_op | source)
XLA Modules:
  0.0 58.3 jit_solution(12956945939851120250)
XLA Ops:
  1.3 0.0 copy-start
  1.3 1.5 %copy-done = f32[1,224,2048]{2,1,0:T(8,128)S(1)} copy-done((f32[1,224,2048]{2,1,0:T(8,128)S(1)}, f32[1,224,2048]{2,1,0:T(8,128)}, u32[]{:S(2)}) %copy-start) | copy-done | bytes 1835032
  2.8 0.0 copy-start.1
  2.8 1.0 %copy-done.1 = f32[1,64,2048]{2,1,0:T(8,128)S(1)} copy-done((f32[1,64,2048]{2,1,0:T(8,128)S(1)}, f32[1,64,2048]{2,1,0:T(8,128)}, u32[]{:S(2)}) %copy-start.1) | copy-done | bytes 524312
  3.8 52.6 %shard_map.50 = (f32[1,224,2048]{2,1,0:T(8,128)S(1)}, f32[8,128]{1,0:T(8,128)S(1)}) custom-call(f32[1,64,2048]{2,1,0:T(8,128)S(1)} %copy-done.1, f32[1,224,2048]{2,1,0:T(8,128)S(1)} %copy-done, s32[1]{0:T(128)S(6)} %copy.6.sup_in), custom_call_target="tpu_custom_call" | custom-call | tf_op jit(solution)/shard_map/pallas_call | solution.py:442
  56.5 0.6 %pad_maximum_fusion = f32[224]{0:T(256)} fusion(f32[64]{0:T(128)S(1)} %get-tuple-element.9, f32[64]{0:T(128)S(1)} %get-tuple-element.8, f32[48]{0:T(128)S(1)} %get-tuple-element.7, f32[48]{0:T(128)S(1)} %get-tuple-element.6), kind=kLoop, calls=%fused_computation | loop fusion | flops 672 | bytes 1792 | tf_op jit(solution)/shard_map/concatenate | solution.py:479
  57.1 1.2 %copy.7 = f32[1,224,2048]{2,1,0:T(8,128)} copy(f32[1,224,2048]{2,1,0:T(8,128)S(1)} %get-tuple-element.12) | data formatting | bytes 3670016
  (2 shorter events, 0.0 us)
Async XLA Ops:
  1.3 1.5 %copy-start = (f32[1,224,2048]{2,1,0:T(8,128)S(1)}, f32[1,224,2048]{2,1,0:T(8,128)}, u32[]{:S(2)}) copy-start(f32[1,224,2048]{2,1,0:T(8,128)} %pot_hbm.1) | copy-start | bytes 5505028
  2.8 1.0 %copy-start.1 = (f32[1,64,2048]{2,1,0:T(8,128)S(1)}, f32[1,64,2048]{2,1,0:T(8,128)}, u32[]{:S(2)}) copy-start(f32[1,64,2048]{2,1,0:T(8,128)} %pts_hbm.1) | copy-start | bytes 1572868

commit v3 on v2

--- a/solution.py
+++ b/solution.py
@@ -473,7 +473,7 @@
             pltpu.SemaphoreType.DMA((3,)),
         ],
         compiler_params=pltpu.CompilerParams(
-            collective_id=0, has_side_effects=True, vmem_limit_bytes=48 * 1024 * 1024),
+            collective_id=0, has_side_effects=True, vmem_limit_bytes=62 * 1024 * 1024),
     )(points, potentials, supports)
     ends = starts[1:] + [cols]
     log_scale = jnp.concatenate(

time: 58.5 us -> 60.6 us (1.036)
  Pallas kernels: 52.6 us -> 54 us
  local copies, waits for them, and re-layouts: 3.77 us -> 4.43 us
    squeeze x2, local copies, waits for them, and re-layouts: 0.01 us -> 1.5 us  [per_device(): logs[b, 0:ends[b] - starts[b]]]
    pallas_call x1, Pallas kernels: 52.6 us -> 54 us  [per_device(): pl.pallas_call(functools.partial(kernel, n_tm, starts, half), out_shape=(...]
    unnamed x5 -> x1, local copies, waits for them, and re-layouts: 3.76 us -> 2.93 us
where the time goes in v3:
time: 60.6 us; the launch traced here: 60.3 us
  Pallas kernels  54 us (89%)
  local copies, waits for them, and re-layouts  4.43 us (7%)
  between operations  1.29 us (2%)
  other arithmetic  0.64 us (1%)
    pallas_call x1, Pallas kernels, per_device(): pl.pallas_call(functools.partial(kernel, n_tm, starts, half), out_shape=(...  54 us
    unnamed x1, local copies, waits for them, and re-layouts  2.93 us
    squeeze x2, local copies, waits for them, and re-layouts, per_device(): logs[b, 0:ends[b] - starts[b]]  1.5 us

profile of v3, /device:TPU:0, one launch (start us, length us, event | category | flops | bytes accessed | tf_op | source)
XLA Modules:
  0.0 60.3 jit_solution(14816925139652591151)
XLA Ops:
  1.3 54.0 %shard_map.50 = (f32[1,224,2048]{2,1,0:T(8,128)}, f32[8,128]{1,0:T(8,128)}) custom-call(f32[1,64,2048]{2,1,0:T(8,128)} %pts_hbm.1, f32[1,224,2048]{2,1,0:T(8,128)} %pot_hbm.1, s32[1]{0:T(128)S(6)} %copy.6.sup_in), custom_call_target="tpu_custom_call" | custom-call | tf_op jit(solution)/shard_map/pallas_call | solution.py:442
  55.2 0.8 %slice_bitcast_fusion.3 = (f32[48]{0:T(128)S(1)}, f32[48]{0:T(128)S(1)}) fusion(f32[8,128]{1,0:T(8,128)} %get-tuple-element.5), kind=kLoop, calls=%fused_computation.4 | loop fusion | bytes 768 | tf_op jit(solution)/shard_map/squeeze | solution.py:480
  56.0 0.7 %slice_bitcast_fusion.1 = (f32[64]{0:T(128)S(1)}, f32[64]{0:T(128)S(1)}) fusion(f32[8,128]{1,0:T(8,128)} %get-tuple-element.5), kind=kLoop, calls=%fused_computation.2 | loop fusion | bytes 1024 | tf_op jit(solution)/shard_map/squeeze | solution.py:480
  56.7 0.6 %pad_maximum_fusion = f32[224]{0:T(256)} fusion(f32[64]{0:T(128)S(1)} %get-tuple-element.9, f32[64]{0:T(128)S(1)} %get-tuple-element.8, f32[48]{0:T(128)S(1)} %get-tuple-element.7, f32[48]{0:T(128)S(1)} %get-tuple-element.6), kind=kLoop, calls=%fused_computation | loop fusion | flops 672 | bytes 1792 | tf_op jit(solution)/shard_map/concatenate | solution.py:479
  57.4 2.9 %copy.7 = f32[1,224,2048]{2,1,0:T(8,128)} copy(f32[1,224,2048]{2,1,0:T(8,128)} %get-tuple-element.12) | data formatting | bytes 3670016
